TPU v7x, 32 devices: a whole 2x2x4 slice. The times are simulated.
32 devices in a mesh: groups: 2 (over y), zone: 4 (over z), scen: 2 (over x), hour: 2 (over core).
Axes of the slice: x: 2, y: 2, z: 4, core: 2. Of those that a mesh axis runs over, the one named last changes fastest.
Arguments:
- forcing: bfloat16 [1024, 48, 64], P(('groups', 'zone', 'scen', 'hour')), parts along dimension 0, may hold values from -3 to 3
- response: bfloat16 [48, 64, 8192], P('hour', None, ('groups', 'zone')), parts along dimension 2, may hold values from -0.75 to 0.75
- window_params: float32 [128, 64], P('groups'), parts along dimension 0, may hold values from 0.5 to 1.5
- building_map: int32 [8192], P(('groups', 'zone')), parts along dimension 0, may hold values from 0 to 1023
- owner_ids: int32 [2048], P('groups'), parts along dimension 0, may hold values from 0 to 63
- band_ids: int32 [48, 8192], P('hour', ('groups', 'zone')), parts along dimension 1, may hold values from 0 to 7
- floor_area: float32 [8192], P(('groups', 'zone')), parts along dimension 0, may hold values from 0.5 to 18, as said below
Outputs:
- sensitivity: float32 [128, 64], P(('groups', 'zone', 'scen', 'hour')), parts along dimension 0
- objective: float32 [2], P('groups'), parts along dimension 0
There are 2 independent parts, one for each index of `groups`. A program takes and returns all parts, laid end to end along the dimension named above; each array names one. Nothing has to cross between parts.
Inputs may be any that keep to these rules, and one draw needn't show every extreme that they name: `floor_area`: floor areas are positive.
All inputs are finite; a program needn't handle non-finite values.
Results may differ from a plain program's by a relative error of at most 0.0006.
Values may be sent and summed in bfloat16 or wider, within the bound.
A program may use at most 128 MiB of HBM per device.

v0:
```python
import math
import jax
import jax.numpy as jnp
from jax import lax
from jax.sharding import PartitionSpec as P

SHARPNESS = 200.0


def joined(value, axis, join):
    pieces = jax.tree.map(lambda part: lax.all_gather(part, axis), value)
    head = jax.tree.map(lambda part: part[0], pieces)
    tail = jax.tree.map(lambda part: part[1:], pieces)
    running, _ = lax.scan(lambda running, share: (join(running, share), None), head, tail)
    return running


def merge_softmax(first, second):
    highest = jnp.maximum(first[0], second[0])
    return (
        highest,
        first[1] * jnp.exp(first[0] - highest) + second[1] * jnp.exp(second[0] - highest),
    )


def on_device(forcing, response, window_params, building_map, owner_ids, band_ids, floor_area):
    hour_local = response.shape[0]
    width = response.shape[1]
    zone_local = response.shape[2]
    hours_total = hour_local * lax.axis_size("hour")
    hour_first = lax.axis_index("hour") * hour_local
    positions = (hour_first + jnp.arange(hour_local)).astype(jnp.float32)
    occupant_level = 1.0 + 2.0 * positions / (hours_total - 1)
    candidate_plan = jnp.take(owner_ids, building_map)
    zone_parameters = jnp.take(window_params, candidate_plan, axis=0)
    coeff = (response.astype(jnp.float32) * zone_parameters.T[None, :, :]).astype(jnp.bfloat16)
    band_low = 0.25 * (band_ids.astype(jnp.float32) - 3.5) - 0.5
    band_high = band_low + 1.0
    zone_weight = occupant_level[:, None] * floor_area[None, :]
    block_count = hour_local // 8
    mine = lax.all_to_all(forcing, "hour", split_axis=1, concat_axis=0, tiled=True)

    def inside_climate_state(outlook_records, initial_clock_time):
        record_elements = lax.slice_in_dim(
            outlook_records, initial_clock_time, initial_clock_time + 8, axis=1
        )
        thermal_demand = jnp.einsum(
            "shp,hpz->hsz",
            record_elements,
            coeff[initial_clock_time : initial_clock_time + 8],
            preferred_element_type=jnp.float32,
        )
        return (thermal_demand, record_elements)

    weight_part = (jnp.sum(floor_area) * jnp.sum(occupant_level)).reshape(1)
    outlook_records = lax.all_gather(mine, "zone", axis=0, tiled=True)
    sums = jnp.zeros((outlook_records.shape[0],), jnp.float32)
    for hour_block in range(block_count):
        initial_clock_time = hour_block * 8
        thermal_demand, record_elements = inside_climate_state(outlook_records, initial_clock_time)
        low = band_low[initial_clock_time : initial_clock_time + 8][:, None, :]
        high = band_high[initial_clock_time : initial_clock_time + 8][:, None, :]
        penalty = jax.nn.softplus(thermal_demand - high) + jax.nn.softplus(low - thermal_demand)
        sums = sums + jnp.sum(
            penalty * zone_weight[initial_clock_time : initial_clock_time + 8][:, None, :],
            axis=(0, 2),
        )
    loss_sum, weight_total = lax.psum((sums, weight_part), ("zone", "hour"))
    scores = SHARPNESS * loss_sum / weight_total[0]
    local_peak = jnp.max(scores)
    peak_score, exp_total = joined(
        (local_peak, jnp.sum(jnp.exp(scores - local_peak))), "scen", merge_softmax
    )
    objective = ((peak_score + jnp.log(exp_total)) / SHARPNESS).reshape(1)
    scen_weight = jnp.exp(scores - peak_score) / exp_total / weight_total[0]
    empty = jnp.zeros((width, zone_local), jnp.float32)
    accumulated = empty
    outlook_records = lax.all_gather(mine, "zone", axis=0, tiled=True)
    for hour_block in range(block_count):
        initial_clock_time = hour_block * 8
        thermal_demand, record_elements = inside_climate_state(outlook_records, initial_clock_time)
        low = band_low[initial_clock_time : initial_clock_time + 8][:, None, :]
        high = band_high[initial_clock_time : initial_clock_time + 8][:, None, :]
        slope = jax.nn.sigmoid(thermal_demand - high) - jax.nn.sigmoid(low - thermal_demand)
        adjoint = (
            slope
            * scen_weight[None, :, None]
            * zone_weight[initial_clock_time : initial_clock_time + 8][:, None, :]
        ).astype(jnp.bfloat16)
        mixed = jnp.einsum(
            "shp,hsz->hpz", record_elements, adjoint, preferred_element_type=jnp.float32
        )
        accumulated = accumulated + jnp.sum(
            response[initial_clock_time : initial_clock_time + 8].astype(jnp.float32) * mixed,
            axis=0,
        )
    zones_all = zone_local * lax.axis_size("zone")
    designs = window_params.shape[0]
    gain = math.sqrt(width * zones_all * hours_total * designs)
    zone_rows = accumulated.T
    owners_local = designs // (
        lax.axis_size("zone") * lax.axis_size("scen") * lax.axis_size("hour")
    )
    onehot = (
        candidate_plan[:, None]
        == jnp.arange(owners_local * lax.axis_size(("zone", "scen", "hour")))[None, :]
    ).astype(jnp.float32)
    sensitivity = lax.psum_scatter(
        gain * jnp.dot(onehot.T, zone_rows, precision=lax.Precision.HIGHEST),
        ("zone", "scen", "hour"),
        scatter_dimension=0,
        tiled=True,
    )
    return (sensitivity, objective)


def solution(mesh):
    in_specs = (
        P(("groups", "zone", "scen", "hour"), None, None),
        P("hour", None, ("groups", "zone")),
        P("groups", None),
        P(("groups", "zone")),
        P("groups"),
        P("hour", ("groups", "zone")),
        P(("groups", "zone")),
    )
    out_specs = (P(("groups", "zone", "scen", "hour"), None), P("groups"))
    return jax.shard_map(
        on_device, mesh=mesh, in_specs=in_specs, out_specs=out_specs, check_vma=False
    )
```

profile of v0, /device:TPU:0, one launch (start us, length us, event | category | flops | bytes accessed | tf_op | source)
XLA Modules:
  0.0 207.4 jit_solution(13071616913442641954)
XLA Ops:
  0.7 1.2 copy.37
  1.8 1.0 reshape.77
  2.9 3.4 %all-to-all-start = ((bf16[2,2,24576]{2,1,0:T(2,128)(2,1)}), bf16[2,2,24576]{2,1,0:T(2,128)(2,1)S(1)}, u32[]{:S(2)}, u32[]{:S(2)}) async-start(bf16[2,2,24576]{2,1,0:T(2,128)(2,1)} %reshape.77), calls=%async_computation | async-start | bytes 393216 | tf_op jit(solution)/shard_map/all_to_all | solution.py:41
  6.3 1.5 all-to-all-done
  8.2 31.7 %all_gather.16 = bf16[256,24,64]{2,1,0:T(8,128)(2,1)S(1)} all-gather(bf16[64,24,64]{2,1,0:T(8,128)(2,1)S(1)} %bitcast.231), channel_id=1, replica_groups=mesh['groups'=2,'zone'=4,'scen'=2,'hour'=2] {'zone'}, dimensions={0}, use_global_device_ids=true | all-gather | bytes 983040 | tf_op jit(solution)/shard_map/all_gather | solution.py:78
  40.6 0.6 multiply_add_fusion
  41.3 4.5 %gather_fusion = s32[1024]{0:T(1024)S(1)} fusion(s32[1024]{0:T(1024)S(1)} %copy-done.1, s32[1024]{0:T(1024)S(1)} %fusion.88), kind=kCustom, calls=%fused_computation | custom fusion | bytes 12288 | tf_op jit(solution)/shard_map/jit(_take)/gather | solution.py:34
  45.9 2.8 %gather_fusion.1 = f32[1024,64]{1,0:T(8,128)S(1)} fusion(f32[64,64]{1,0:T(8,128)S(1)} %copy-done, s32[1024]{0:T(1024)S(1)} %fusion.89), kind=kCustom, calls=%fused_computation.1 | custom fusion | bytes 528384 | tf_op jit(solution)/shard_map/jit(_take)/gather | solution.py:35
  49.8 0.6 reduce_sum.84
  51.7 13.8 %fusion.8 = (f32[256]{0:T(256)S(1)}, f32[8,1024,256]{2,1,0:T(8,128)}) fusion(f32[8,1024]{1,0:T(8,128)S(1)} %get-tuple-element.35, f32[8,1024]{1,0:T(8,128)S(1)} %get-tuple-element.52, f32[8,1024]{1,0:T(8,128)S(1)} %get-tuple-element.29, bf16[256,8,64]{0,2,1:T(8,128)(2,1)S(1)} %copy.35, bf16[24,64,1024]{2,1,0:T(8,128)(2,1)} %param.8, f32[64,1024]{1,0:T(8,128)S(1)} %copy.19), kind=kOutput, calls=%fused_computation.16 | convolution fusion | flops 308805376 | bytes 12157952 | tf_op jit(solution)/shard_map/shp,hpz->hsz/dot_general | solution.py:47
  65.5 13.3 %fusion.2 = (f32[256]{0:T(256)S(1)}, f32[8,1024,256]{2,1,0:T(8,128)}) fusion(f32[8,1024]{1,0:T(8,128)S(1)} %get-tuple-element.36, f32[8,1024]{1,0:T(8,128)S(1)} %get-tuple-element.51, f32[8,1024]{1,0:T(8,128)S(1)} %get-tuple-element.30, bf16[256,8,64]{0,2,1:T(8,128)(2,1)S(1)} %copy.33, bf16[24,64,1024]{2,1,0:T(8,128)(2,1)S(1)} %copy-done.5, ...), kind=kOutput, calls=%fused_computation.10 | convolution fusion | flops 308805376 | bytes 12157952 | tf_op jit(solution)/shard_map/shp,hpz->hsz/dot_general | solution.py:47
  78.8 13.2 %fusion.5 = (f32[256]{0:T(256)S(1)}, f32[8,1024,256]{2,1,0:T(8,128)}) fusion(f32[8,1024]{1,0:T(8,128)S(1)} %get-tuple-element.34, f32[8,1024]{1,0:T(8,128)S(1)} %get-tuple-element.53, f32[8,1024]{1,0:T(8,128)S(1)} %get-tuple-element.28, bf16[256,8,64]{0,2,1:T(8,128)(2,1)S(1)} %copy.34, bf16[24,64,1024]{2,1,0:T(8,128)(2,1)S(1)} %copy-done.5, ...), kind=kOutput, calls=%fused_computation.13 | convolution fusion | flops 308805376 | bytes 12157952 | tf_op jit(solution)/shard_map/shp,hpz->hsz/dot_general | solution.py:47
  92.0 16.5 %all-reduce.3 = (f32[256]{0:T(256)S(1)}, f32[]{:T(128)}) all-reduce(f32[256]{0:T(256)S(1)} %add_add_fusion, f32[]{:T(128)S(6)} %mul.142), channel_id=1, replica_groups=mesh['groups'=2,'zone'=4,'scen'=2,'hour'=2] {'zone','hour'}, use_global_device_ids=true, to_apply=%region_3.4 | all-reduce | flops 257 | bytes 2056 | tf_op jit(solution)/shard_map/psum | solution.py:68
  108.5 1.2 fusion.94
  109.8 1.3 exponential_reduce_fusion
  111.6 1.3 dynamic-update-slice.1
  112.9 1.3 dynamic-update-slice
  114.2 5.1 %all-reduce.4 = (f32[2]{0:T(128)S(1)}, f32[2]{0:T(128)S(1)}) all-reduce(f32[2]{0:T(128)S(1)} %dynamic-update-slice.1, f32[2]{0:T(128)S(1)} %dynamic-update-slice), channel_id=1, replica_groups=mesh['groups'=2,'zone'=4,'scen'=2,'hour'=2] {'scen'}, use_global_device_ids=true, to_apply=%add.1 | all-reduce | flops 4 | bytes 32
  119.3 0.6 fusion.100
  125.1 8.3 %fusion.72 = f32[64,1024]{1,0:T(8,128)S(1)} fusion(bf16[256,8,64]{0,2,1:T(8,128)(2,1)S(1)} %copy.35, f32[8,1024,256]{2,1,0:T(8,128)} %get-tuple-element.44, f32[256]{0:T(256)S(1)} %exponential_divide_fusion, f32[8,1024]{1,0:T(8,128)S(1)} %get-tuple-element.35, f32[8,1024]{1,0:T(8,128)S(1)} %get-tuple-element.52, f32[8,1024]{1,0:T(8,128)S(1)} %get-tuple-element.29, ...), kind=kOutput, calls=%fused_computation.97 | convolution fusion | flops 295108608 | bytes 10060800 | tf_op jit(solution)/shard_map/shp,hsz->hpz/dot_general | solution.py:90
  133.5 6.3 %fusion.74 = f32[64,1024]{1,0:T(8,128)S(1)} fusion(bf16[256,8,64]{0,2,1:T(8,128)(2,1)S(1)} %copy.33, f32[8,1024,256]{2,1,0:T(8,128)S(1)} %copy-done.9, f32[256]{0:T(256)S(1)} %exponential_divide_fusion, f32[8,1024]{1,0:T(8,128)S(1)} %get-tuple-element.36, f32[8,1024]{1,0:T(8,128)S(1)} %get-tuple-element.51, f32[8,1024]{1,0:T(8,128)S(1)} %get-tuple-element.30, ...), kind=kOutput, calls=%fused_computation.101 | convolution fusion | flops 295108608 | bytes 10060800 | tf_op jit(solution)/shard_map/shp,hsz->hpz/dot_general | solution.py:90
  139.9 6.3 %fusion.73 = f32[64,1024]{1,0:T(8,128)S(1)} fusion(bf16[256,8,64]{0,2,1:T(8,128)(2,1)S(1)} %copy.34, f32[8,1024,256]{2,1,0:T(8,128)S(1)} %bitcast.233, f32[256]{0:T(256)S(1)} %exponential_divide_fusion, f32[8,1024]{1,0:T(8,128)S(1)} %get-tuple-element.34, f32[8,1024]{1,0:T(8,128)S(1)} %get-tuple-element.53, f32[8,1024]{1,0:T(8,128)S(1)} %get-tuple-element.28, ...), kind=kOutput, calls=%fused_computation.99 | convolution fusion | flops 295108608 | bytes 10060800 | tf_op jit(solution)/shard_map/shp,hsz->hpz/dot_general | solution.py:90
  146.2 0.6 convolution_multiply_fusion
  146.8 57.6 %all-reduce.2 = f32[64,64]{1,0:T(8,128)S(1)} all-reduce(f32[64,64]{1,0:T(8,128)S(1)} %convolution_multiply_fusion), channel_id=2, replica_groups=mesh['groups'=2,'zone'=4,'scen'=2,'hour'=2] {'zone','scen','hour'}, use_global_device_ids=true, to_apply=%region_12.13.clone | all-reduce | flops 4096 | bytes 32768
  (48 shorter events, 4.6 us)
Async XLA Ops:
  0.6 45.3 %copy-start = (f32[64,64]{1,0:T(8,128)S(1)}, f32[64,64]{1,0:T(8,128)}, u32[]{:S(2)}) copy-start(f32[64,64]{1,0:T(8,128)} %param.9) | copy-start | bytes 49156
  0.6 40.5 %copy-start.3 = (f32[1024]{0:T(1024)S(1)}, f32[1024]{0:T(1024)}, u32[]{:S(2)}) copy-start(f32[1024]{0:T(1024)} %param.13) | copy-start | bytes 12292
  0.7 40.6 %copy-start.2 = (s32[24,1024]{1,0:T(8,128)S(1)}, s32[24,1024]{1,0:T(8,128)}, u32[]{:S(2)}) copy-start(s32[24,1024]{1,0:T(8,128)} %param.12) | copy-start | bytes 294916
  0.7 40.6 %copy-start.4 = (s32[1024]{0:T(1024)S(1)}, s32[1024]{0:T(1024)}, u32[]{:S(2)}) copy-start(s32[1024]{0:T(1024)} %param.10) | copy-start | bytes 12292
  0.7 40.7 %copy-start.1 = (s32[1024]{0:T(1024)S(1)}, s32[1024]{0:T(1024)}, u32[]{:S(2)}) copy-start(s32[1024]{0:T(1024)} %param.11) | copy-start | bytes 12292
  2.9 4.9 %all-to-all-start = ((bf16[2,2,24576]{2,1,0:T(2,128)(2,1)}), bf16[2,2,24576]{2,1,0:T(2,128)(2,1)S(1)}, u32[]{:S(2)}, u32[]{:S(2)}) async-start(bf16[2,2,24576]{2,1,0:T(2,128)(2,1)} %reshape.77), calls=%async_computation | async-start | bytes 393216 | tf_op jit(solution)/shard_map/all_to_all | solution.py:41
  51.7 13.8 %copy-start.5 = (bf16[24,64,1024]{2,1,0:T(8,128)(2,1)S(1)}, bf16[24,64,1024]{2,1,0:T(8,128)(2,1)}, u32[]{:S(2)}) copy-start(bf16[24,64,1024]{2,1,0:T(8,128)(2,1)} %param.8) | copy-start | bytes 9437188
  78.8 32.3 %copy-start.8 = (u32[32]{0:T(128)S(1)}, u32[32]{0:T(128)}, u32[]{:S(2)}) copy-start(u32[32]{0:T(128)} %constant.81) | copy-start | bytes 388
  125.1 8.4 %copy-start.6 = (bf16[24,64,1024]{2,1,0:T(8,128)(2,1)S(1)}, bf16[24,64,1024]{2,1,0:T(8,128)(2,1)}, u32[]{:S(2)}) copy-start(bf16[24,64,1024]{2,1,0:T(8,128)(2,1)} %param.8) | copy-start | bytes 9437188
  125.1 8.3 %copy-start.9 = (f32[8,1024,256]{2,1,0:T(8,128)S(1)}, f32[8,1024,256]{2,1,0:T(8,128)}, u32[]{:S(2)}) copy-start(f32[8,1024,256]{2,1,0:T(8,128)} %get-tuple-element.46) | copy-start | bytes 25165828
  125.1 14.7 %slice-start = ((s8[8388608]{0:T(1024)(128)(4,1)}), s8[4194304]{0:T(1024)(128)(4,1)S(1)}, s32[]{:S(2)}) async-start(s8[8388608]{0:T(1024)(128)(4,1)} %bitcast.232), calls=%async_computation.1 | async-start | bytes 8388608
  133.5 6.4 %slice-start.1 = ((s8[8388608]{0:T(1024)(128)(4,1)}), s8[4194304]{0:T(1024)(128)(4,1)S(1)}, s32[]{:S(2)}) async-start(s8[8388608]{0:T(1024)(128)(4,1)} %bitcast.232), calls=%async_computation.2 | async-start | bytes 8388608
  139.9 64.6 %copy-start.7 = (u32[32]{0:T(128)S(1)}, u32[32]{0:T(128)}, u32[]{:S(2)}) copy-start(u32[32]{0:T(128)} %constant.93) | copy-start | bytes 388
where the time goes:
time: 208 us; the launch traced here: 207 us
  blocking collectives  111 us (53%)
  matrix products  61.8 us (30%)
  local copies, waits for them, and re-layouts  17 us (8%)
  between operations  8.65 us (4%)
  other arithmetic  4.05 us (2%)
  starting transfers between devices  3.43 us (2%)
    unnamed x2, blocking collectives  62.7 us
    dot_general x3, matrix products, inside_climate_state(): jnp.einsum('shp,hpz->hsz', record_elements, coeff[initial_clock_time:init...  40.3 us
    all_gather x1, blocking collectives, on_device(): outlook_records = lax.all_gather(mine, 'zone', axis=0, tiled=True)  31.7 us
    dot_general x3, matrix products, on_device(): jnp.einsum('shp,hsz->hpz', record_elements, adjoint, preferred_element_ty...  20.9 us
    psum x1, blocking collectives, on_device(): loss_sum, weight_total = lax.psum((sums, weight_part), ('zone', 'hour'))  16.5 us
    unnamed x37, local copies, waits for them, and re-layouts  7.84 us
    gather x1, local copies, waits for them, and re-layouts, on_device(): candidate_plan = jnp.take(owner_ids, building_map)  4.53 us
  transfers between devices with their start and end apart: 1, of which 1 were waited for; matrix products, arithmetic and copies ran while one was open for 0% of the time, Pallas kernels for 0%

commit v1 on v0

--- a/solution.py
+++ b/solution.py
@@ -75,7 +75,12 @@
     scen_weight = jnp.exp(scores - peak_score) / exp_total / weight_total[0]
     empty = jnp.zeros((width, zone_local), jnp.float32)
     accumulated = empty
-    outlook_records = lax.all_gather(mine, "zone", axis=0, tiled=True)
+    ring = [mine]
+    for hop in range(3):
+        ring.append(lax.ppermute(ring[-1], "zone", [(dev, (dev + 1) % 4) for dev in range(4)]))
+    outlook_records = jnp.roll(
+        jnp.concatenate(ring[::-1], axis=0), (lax.axis_index("zone") + 1) * ring[0].shape[0], axis=0
+    )
     for hour_block in range(block_count):
         initial_clock_time = hour_block * 8
         thermal_demand, record_elements = inside_climate_state(outlook_records, initial_clock_time)

time: 208 us -> 232 us (1.12)
  waiting for transfers between devices: 1.49 us -> 14.6 us
  matrix products: 61.8 us -> 54.9 us
  other arithmetic: 4.05 us -> 10.2 us
  blocking collectives: 111 us -> 117 us
  local copies, waits for them, and re-layouts: 17 us -> 22 us
    ppermute x0 -> x3, waiting for transfers between devices: none -> 14.6 us  [on_device(): lax.ppermute(ring[-1], 'zone', [(dev, (dev + 1) % 4) for dev in range(4)])]
    dot_general x3, matrix products: 20.9 us -> 14.9 us  [on_device(): jnp.einsum('shp,hsz->hpz', record_elements, adjoint, preferred_element_ty...]
    all_gather x1, blocking collectives: 31.7 us -> 36.7 us  [on_device(): outlook_records = lax.all_gather(mine, 'zone', axis=0, tiled=True)]
    convert_element_type x0 -> x1, other arithmetic: none -> 4.51 us  [on_device(): (response.astype(jnp.float32) * zone_parameters.T[None, :, :]).astype(jnp...]
    concatenate x0 -> x1, local copies, waits for them, and re-layouts: none -> 4.24 us  [on_device(): jnp.roll(jnp.concatenate(ring[::-1], axis=0), (lax.axis_index('zone') + 1...]
    all_to_all x0 -> x1, blocking collectives: none -> 3.89 us  [on_device(): lax.all_to_all(forcing, 'hour', split_axis=1, concat_axis=0, tiled=True)]
    all_to_all x1 -> x0, starting transfers between devices: 3.43 us -> none  [on_device(): lax.all_to_all(forcing, 'hour', split_axis=1, concat_axis=0, tiled=True)]
    ppermute x0 -> x3, starting transfers between devices: none -> 3.08 us  [on_device(): lax.ppermute(ring[-1], 'zone', [(dev, (dev + 1) % 4) for dev in range(4)])]
  transfers between devices with their start and end apart: 1 -> 3, of which waited for: 1 -> 2; matrix products, arithmetic and copies ran while one was open for 0% -> 25% of each run, Pallas kernels for 0% -> 0%
where the time goes in v1:
time: 232 us; the launch traced here: 231 us
  blocking collectives  117 us (50%)
  matrix products  54.9 us (24%)
  local copies, waits for them, and re-layouts  22 us (9%)
  waiting for transfers between devices  14.6 us (6%)
  other arithmetic  10.2 us (4%)
  between operations  9.09 us (4%)
  starting transfers between devices  3.08 us (1%)
    unnamed x2, blocking collectives  62.5 us
    dot_general x6, matrix products, inside_climate_state(): jnp.einsum('shp,hpz->hsz', record_elements, coeff[initial_clock_time:init...  39.4 us
    all_gather x1, blocking collectives, on_device(): outlook_records = lax.all_gather(mine, 'zone', axis=0, tiled=True)  36.7 us
    dot_general x3, matrix products, on_device(): jnp.einsum('shp,hsz->hpz', record_elements, adjoint, preferred_element_ty...  14.9 us
    ppermute x3, waiting for transfers between devices, on_device(): lax.ppermute(ring[-1], 'zone', [(dev, (dev + 1) % 4) for dev in range(4)])  14.6 us
    psum x1, blocking collectives, on_device(): loss_sum, weight_total = lax.psum((sums, weight_part), ('zone', 'hour'))  14.2 us
    unnamed x64, local copies, waits for them, and re-layouts  6.73 us
  transfers between devices with their start and end apart: 3, of which 2 were waited for; matrix products, arithmetic and copies ran while one was open for 25% of the time, Pallas kernels for 0%

profile of v1, /device:TPU:0, one launch (start us, length us, event | category | flops | bytes accessed | tf_op | source)
XLA Modules:
  0.0 231.3 jit_solution(2776987669019500715)
XLA Ops:
  2.1 3.9 %all_to_all.18 = bf16[2,2,24576]{2,1,0:T(2,128)(2,1)S(1)} all-to-all(bf16[2,2,24576]{2,1,0:T(2,128)(2,1)S(1)} %reshape.77), channel_id=1, replica_groups=mesh['groups'=2,'zone'=4,'scen'=2,'hour'=2] {'hour'}, dimensions={0} | all-to-all | bytes 393216 | tf_op jit(solution)/shard_map/all_to_all | solution.py:41
  6.8 3.1 %collective-permute-start = (bf16[64,24,64]{0,2,1:T(8,128)(2,1)S(1)}, bf16[64,24,64]{0,2,1:T(8,128)(2,1)S(1)}, u32[]{:S(2)}, u32[]{:S(2)}) collective-permute-start(bf16[64,24,64]{0,2,1:T(8,128)(2,1)S(1)} %copy.43), channel_id=1, source_target_pairs={{0,4},{4,8},{8,12},{12,0},{1,5},{5,9},{9,13},{13,1},{2,6},{6,10},{... | collective-permute-start | bytes 589832 | tf_op jit(solution)/shard_map/ppermute | solution.py:80
  9.8 36.7 %all_gather.15 = bf16[256,24,64]{2,1,0:T(8,128)(2,1)S(1)} all-gather(bf16[64,24,64]{2,1,0:T(8,128)(2,1)S(1)} %bitcast.119), channel_id=1, replica_groups=mesh['groups'=2,'zone'=4,'scen'=2,'hour'=2] {'zone'}, dimensions={0}, use_global_device_ids=true | all-gather | bytes 983040 | tf_op jit(solution)/shard_map/all_gather | solution.py:56
  47.3 4.5 %gather_fusion = s32[1024]{0:T(1024)S(1)} fusion(s32[1024]{0:T(1024)S(1)} %copy-done.1, s32[1024]{0:T(1024)S(1)} %fusion.58), kind=kCustom, calls=%fused_computation | custom fusion | bytes 12288 | tf_op jit(solution)/shard_map/jit(_take)/gather | solution.py:34
  51.9 2.8 %gather_fusion.1 = f32[1024,64]{1,0:T(8,128)S(1)} fusion(f32[64,64]{1,0:T(8,128)S(1)} %copy-done, s32[1024]{0:T(1024)S(1)} %fusion.59), kind=kCustom, calls=%fused_computation.1 | custom fusion | bytes 528384 | tf_op jit(solution)/shard_map/jit(_take)/gather | solution.py:35
  59.2 4.5 %multiply_convert_fusion.3 = bf16[24,64,1024]{2,1,0:T(8,128)(2,1)} fusion(bf16[24,64,1024]{2,1,0:T(8,128)(2,1)} %param.8, f32[64,1024]{1,0:T(8,128)S(1)} %copy.46), kind=kLoop, calls=%fused_computation.56 | loop fusion | flops 4718592 | bytes 6553600 | tf_op jit(solution)/shard_map/convert_element_type | solution.py:36
  65.1 12.0 %fusion.2 = f32[256]{0:T(256)S(1)} fusion(f32[8,1024]{1,0:T(8,128)} %get-tuple-element.36, f32[8,1024]{1,0:T(8,128)S(1)} %get-tuple-element.43, f32[8,1024]{1,0:T(8,128)S(1)} %get-tuple-element.30, bf16[24,64,1024]{2,1,0:T(8,128)(2,1)} %multiply_convert_fusion.3, bf16[256,8,64]{2,1,0:T(8,128)(2,1)} %get-tuple-element.26), kind=kOutput, calls=%fused_computation.10 | convolution fusion | flops 304086784 | bytes 3507200 | tf_op jit(solution)/shard_map/shp,hpz->hsz/dot_general | solution.py:47
  77.2 10.8 %fusion.5 = f32[256]{0:T(256)S(1)} fusion(f32[8,1024]{1,0:T(8,128)S(1)} %copy-done.22, f32[8,1024]{1,0:T(8,128)S(1)} %get-tuple-element.45, f32[8,1024]{1,0:T(8,128)S(1)} %get-tuple-element.28, bf16[24,64,1024]{2,1,0:T(8,128)(2,1)S(1)} %copy-done.3, bf16[256,8,64]{2,1,0:T(8,128)(2,1)S(1)} %copy-done.5), kind=kOutput, calls=%fused_computation.13 | convolution fusion | flops 304086784 | bytes 3507200 | tf_op jit(solution)/shard_map/shp,hpz->hsz/dot_general | solution.py:47
  88.0 10.6 %fusion.8 = f32[256]{0:T(256)S(1)} fusion(f32[8,1024]{1,0:T(8,128)S(1)} %copy-done.20, f32[8,1024]{1,0:T(8,128)S(1)} %get-tuple-element.44, f32[8,1024]{1,0:T(8,128)S(1)} %get-tuple-element.29, bf16[24,64,1024]{2,1,0:T(8,128)(2,1)S(1)} %copy-done.3, bf16[256,8,64]{2,1,0:T(8,128)(2,1)S(1)} %get-tuple-element.27), kind=kOutput, calls=%fused_computation.16 | convolution fusion | flops 304086784 | bytes 3507200 | tf_op jit(solution)/shard_map/shp,hpz->hsz/dot_general | solution.py:47
  98.7 14.2 %all-reduce.3 = (f32[256]{0:T(256)S(1)}, f32[]{:T(128)}) all-reduce(f32[256]{0:T(256)S(1)} %add_add_fusion, f32[]{:T(128)S(6)} %mul.146), channel_id=1, replica_groups=mesh['groups'=2,'zone'=4,'scen'=2,'hour'=2] {'zone','hour'}, use_global_device_ids=true, to_apply=%region_3.4 | all-reduce | flops 257 | bytes 2056 | tf_op jit(solution)/shard_map/psum | solution.py:68
  114.8 1.4 dynamic-update-slice
  116.2 1.3 exponential_reduce_fusion
  117.5 1.4 dynamic-update-slice.1
  118.9 4.9 %all-reduce.4 = (f32[2]{0:T(128)S(1)}, f32[2]{0:T(128)S(1)}) all-reduce(f32[2]{0:T(128)S(1)} %dynamic-update-slice.1, f32[2]{0:T(128)S(1)} %dynamic-update-slice), channel_id=1, replica_groups=mesh['groups'=2,'zone'=4,'scen'=2,'hour'=2] {'scen'}, use_global_device_ids=true, to_apply=%add.1 | all-reduce | flops 4 | bytes 32
  131.1 4.1 %collective-permute-done.1 = bf16[64,24,64]{0,2,1:T(8,128)(2,1)S(1)} collective-permute-done((bf16[64,24,64]{0,2,1:T(8,128)(2,1)S(1)}, bf16[64,24,64]{0,2,1:T(8,128)(2,1)S(1)}, u32[]{:S(2)}, u32[]{:S(2)}) %collective-permute-start.1) | collective-permute-done | bytes 196640 | tf_op jit(solution)/shard_map/ppermute | solution.py:80
  135.3 10.5 %collective-permute-done.2 = bf16[64,24,64]{0,2,1:T(8,128)(2,1)S(1)} collective-permute-done((bf16[64,24,64]{0,2,1:T(8,128)(2,1)S(1)}, bf16[64,24,64]{0,2,1:T(8,128)(2,1)S(1)}, u32[]{:S(2)}, u32[]{:S(2)}) %collective-permute-start.2) | collective-permute-done | bytes 196640 | tf_op jit(solution)/shard_map/ppermute | solution.py:80
  145.7 4.2 %concatenate.6 = bf16[512,24,64]{0,2,1:T(8,128)(2,1)S(1)} concatenate(bf16[64,24,64]{0,2,1:T(8,128)(2,1)S(1)} %collective-permute-done.2, bf16[64,24,64]{0,2,1:T(8,128)(2,1)S(1)} %collective-permute-done.1, bf16[64,24,64]{0,2,1:T(8,128)(2,1)S(1)} %collective-permute-done, bf16[64,24,64]{0,2,1:T(8,128)(2,1)S(1)} %copy.43, bf16[64,24,64]{0,2,1:T(8,128)(2,1)S(1)} %collective-permute-done.2, ...), dimensions={0} | concatenate | bytes 3145728 | tf_op jit(solution)/shard_map/jit(_roll_dynamic)/concatenate | solution.py:81
  150.0 2.9 %fusion.38 = f32[8,256,1024]{2,1,0:T(8,128)S(1)} fusion(bf16[24,64,1024]{2,1,0:T(8,128)(2,1)} %multiply_convert_fusion.3, bf16[512,24,64]{0,2,1:T(8,128)(2,1)S(1)} %concatenate.6, s32[]{:T(128)S(6)} %select_n.67), kind=kOutput, calls=%fused_computation.66 | convolution fusion | flops 268435456 | bytes 10223620 | tf_op jit(solution)/shard_map/shp,hpz->hsz/dot_general | solution.py:47
  152.9 1.5 fusion.40
  154.5 1.5 fusion.36
  156.4 4.9 %multiply_reduce_fusion.1 = f32[64,1024]{1,0:T(8,128)S(1)} fusion(f32[8,256,1024]{2,1,0:T(8,128)S(1)} %fusion.38, f32[8,1024]{1,0:T(8,128)S(1)} %copy-done.19, f32[8,1024]{1,0:T(8,128)S(1)} %copy-done.17, f32[256]{0:T(256)S(1)} %exponential_divide_fusion, f32[8,1024]{1,0:T(8,128)S(1)} %copy-done.22, bf16[24,64,1024]{2,1,0:T(8,128)(2,1)S(1)} %copy-done.2, ...), kind=kOutput, calls=%fused_computation.61 | convolution fusion | flops 295108608 | bytes 10585092 | tf_op jit(solution)/shard_map/shp,hsz->hpz/dot_general | solution.py:95
  161.3 4.9 %multiply_reduce_fusion.2 = f32[64,1024]{1,0:T(8,128)S(1)} fusion(f32[8,256,1024]{2,1,0:T(8,128)S(1)} %fusion.40, f32[256]{0:T(256)S(1)} %exponential_divide_fusion, f32[8,1024]{1,0:T(8,128)S(1)} %copy-done.21, f32[8,1024]{1,0:T(8,128)S(1)} %copy-done.15, f32[8,1024]{1,0:T(8,128)S(1)} %copy-done.13, bf16[24,64,1024]{2,1,0:T(8,128)(2,1)S(1)} %copy-done.2, ...), kind=kOutput, calls=%fused_computation.62 | convolution fusion | flops 295108608 | bytes 10585092 | tf_op jit(solution)/shard_map/shp,hsz->hpz/dot_general | solution.py:95
  166.2 5.1 %multiply_reduce_fusion = f32[64,1024]{1,0:T(8,128)S(1)} fusion(f32[8,256,1024]{2,1,0:T(8,128)S(1)} %fusion.36, f32[8,1024]{1,0:T(8,128)S(1)} %copy-done.11, f32[8,1024]{1,0:T(8,128)S(1)} %copy-done.9, f32[256]{0:T(256)S(1)} %exponential_divide_fusion, f32[8,1024]{1,0:T(8,128)S(1)} %copy-done.20, bf16[24,64,1024]{2,1,0:T(8,128)(2,1)S(1)} %copy-done.2, ...), kind=kOutput, calls=%fused_computation.60 | convolution fusion | flops 295108608 | bytes 10585092 | tf_op jit(solution)/shard_map/shp,hsz->hpz/dot_general | solution.py:95
  172.0 57.6 %all-reduce.2 = f32[64,64]{1,0:T(8,128)S(1)} all-reduce(f32[64,64]{1,0:T(8,128)S(1)} %convolution_multiply_fusion), channel_id=2, replica_groups=mesh['groups'=2,'zone'=4,'scen'=2,'hour'=2] {'zone','scen','hour'}, use_global_device_ids=true, to_apply=%region_12.13.clone | all-reduce | flops 4096 | bytes 32768
  (85 shorter events, 12.6 us)
Async XLA Ops:
  0.6 51.2 %copy-start = (f32[64,64]{1,0:T(8,128)S(1)}, f32[64,64]{1,0:T(8,128)}, u32[]{:S(2)}) copy-start(f32[64,64]{1,0:T(8,128)} %param.9) | copy-start | bytes 49156
  0.6 51.2 %copy-start.24 = (s32[1024]{0:T(1024)S(1)}, s32[1024]{0:T(1024)}, u32[]{:S(2)}) copy-start(s32[1024]{0:T(1024)} %param.10) | copy-start | bytes 12292
  0.7 46.6 %copy-start.1 = (s32[1024]{0:T(1024)S(1)}, s32[1024]{0:T(1024)}, u32[]{:S(2)}) copy-start(s32[1024]{0:T(1024)} %param.11) | copy-start | bytes 12292
  0.7 56.0 %copy-start.23 = (f32[1024]{0:T(1024)S(1)}, f32[1024]{0:T(1024)}, u32[]{:S(2)}) copy-start(f32[1024]{0:T(1024)} %param.13) | copy-start | bytes 12292
  6.8 117.1 %collective-permute-start = (bf16[64,24,64]{0,2,1:T(8,128)(2,1)S(1)}, bf16[64,24,64]{0,2,1:T(8,128)(2,1)S(1)}, u32[]{:S(2)}, u32[]{:S(2)}) collective-permute-start(bf16[64,24,64]{0,2,1:T(8,128)(2,1)S(1)} %copy.43), channel_id=1, source_target_pairs={{0,4},{4,8},{8,12},{12,0},{1,5},{5,9},{9,13},{13,1},{2,6},{6,10},{... | collective-permute-start | bytes 589832 | tf_op jit(solution)/shard_map/ppermute | solution.py:80
  63.7 13.4 %copy-start.12 = (f32[8,1024]{1,0:T(8,128)}, f32[8,1024]{1,0:T(8,128)S(1)}, u32[]{:S(2)}) copy-start(f32[8,1024]{1,0:T(8,128)S(1)} %get-tuple-element.30) | copy-start | bytes 98308
  63.7 13.4 %copy-start.14 = (f32[8,1024]{1,0:T(8,128)}, f32[8,1024]{1,0:T(8,128)S(1)}, u32[]{:S(2)}) copy-start(f32[8,1024]{1,0:T(8,128)S(1)} %get-tuple-element.43) | copy-start | bytes 98308
  63.7 13.4 %copy-start.16 = (f32[8,1024]{1,0:T(8,128)}, f32[8,1024]{1,0:T(8,128)S(1)}, u32[]{:S(2)}) copy-start(f32[8,1024]{1,0:T(8,128)S(1)} %get-tuple-element.28) | copy-start | bytes 98308
  63.7 13.4 %copy-start.18 = (f32[8,1024]{1,0:T(8,128)}, f32[8,1024]{1,0:T(8,128)S(1)}, u32[]{:S(2)}) copy-start(f32[8,1024]{1,0:T(8,128)S(1)} %get-tuple-element.45) | copy-start | bytes 98308
  63.8 24.2 %copy-start.8 = (f32[8,1024]{1,0:T(8,128)}, f32[8,1024]{1,0:T(8,128)S(1)}, u32[]{:S(2)}) copy-start(f32[8,1024]{1,0:T(8,128)S(1)} %get-tuple-element.29) | copy-start | bytes 98308
  63.8 24.2 %copy-start.10 = (f32[8,1024]{1,0:T(8,128)}, f32[8,1024]{1,0:T(8,128)S(1)}, u32[]{:S(2)}) copy-start(f32[8,1024]{1,0:T(8,128)S(1)} %get-tuple-element.44) | copy-start | bytes 98308
  65.1 12.0 %copy-start.3 = (bf16[24,64,1024]{2,1,0:T(8,128)(2,1)S(1)}, bf16[24,64,1024]{2,1,0:T(8,128)(2,1)}, u32[]{:S(2)}) copy-start(bf16[24,64,1024]{2,1,0:T(8,128)(2,1)} %multiply_convert_fusion.3) | copy-start | bytes 9437188
  65.1 12.0 %copy-start.5 = (bf16[256,8,64]{2,1,0:T(8,128)(2,1)S(1)}, bf16[256,8,64]{2,1,0:T(8,128)(2,1)}, u32[]{:S(2)}) copy-start(bf16[256,8,64]{2,1,0:T(8,128)(2,1)} %get-tuple-element.25) | copy-start | bytes 786436
  65.1 12.0 %copy-start.22 = (f32[8,1024]{1,0:T(8,128)S(1)}, f32[8,1024]{1,0:T(8,128)}, u32[]{:S(2)}) copy-start(f32[8,1024]{1,0:T(8,128)} %get-tuple-element.34) | copy-start | bytes 98308
  77.2 10.8 %copy-start.20 = (f32[8,1024]{1,0:T(8,128)S(1)}, f32[8,1024]{1,0:T(8,128)}, u32[]{:S(2)}) copy-start(f32[8,1024]{1,0:T(8,128)} %get-tuple-element.35) | copy-start | bytes 98308
  88.0 26.2 %copy-start.26 = (u32[32]{0:T(128)S(1)}, u32[32]{0:T(128)}, u32[]{:S(2)}) copy-start(u32[32]{0:T(128)} %constant.110) | copy-start | bytes 388
  88.0 41.9 %copy-start.25 = (u32[32]{0:T(128)S(1)}, u32[32]{0:T(128)}, u32[]{:S(2)}) copy-start(u32[32]{0:T(128)} %constant.122) | copy-start | bytes 388
  123.9 11.4 %collective-permute-start.1 = (bf16[64,24,64]{0,2,1:T(8,128)(2,1)S(1)}, bf16[64,24,64]{0,2,1:T(8,128)(2,1)S(1)}, u32[]{:S(2)}, u32[]{:S(2)}) collective-permute-start(bf16[64,24,64]{0,2,1:T(8,128)(2,1)S(1)} %collective-permute-done), channel_id=1, source_target_pairs={{0,4},{4,8},{8,12},{12,0},{1,5},{5,9},{9,13},{13,1},{2,6},{6,10},{... | collective-permute-start | bytes 589832 | tf_op jit(solution)/shard_map/ppermute | solution.py:80
  135.3 10.5 %collective-permute-start.2 = (bf16[64,24,64]{0,2,1:T(8,128)(2,1)S(1)}, bf16[64,24,64]{0,2,1:T(8,128)(2,1)S(1)}, u32[]{:S(2)}, u32[]{:S(2)}) collective-permute-start(bf16[64,24,64]{0,2,1:T(8,128)(2,1)S(1)} %collective-permute-done.1), channel_id=1, source_target_pairs={{0,4},{4,8},{8,12},{12,0},{1,5},{5,9},{9,13},{13,1},{2,6},{6,10},{... | collective-permute-start | bytes 589832 | tf_op jit(solution)/shard_map/ppermute | solution.py:80
  156.4 4.9 %copy-start.15 = (f32[8,1024]{1,0:T(8,128)S(1)}, f32[8,1024]{1,0:T(8,128)}, u32[]{:S(2)}) copy-start(f32[8,1024]{1,0:T(8,128)} %copy-done.14) | copy-start | bytes 98308
  156.4 4.9 %copy-start.21 = (f32[8,1024]{1,0:T(8,128)S(1)}, f32[8,1024]{1,0:T(8,128)}, u32[]{:S(2)}) copy-start(f32[8,1024]{1,0:T(8,128)} %get-tuple-element.36) | copy-start | bytes 98308
  161.3 4.9 %copy-start.9 = (f32[8,1024]{1,0:T(8,128)S(1)}, f32[8,1024]{1,0:T(8,128)}, u32[]{:S(2)}) copy-start(f32[8,1024]{1,0:T(8,128)} %copy-done.8) | copy-start | bytes 98308
  161.3 4.9 %copy-start.11 = (f32[8,1024]{1,0:T(8,128)S(1)}, f32[8,1024]{1,0:T(8,128)}, u32[]{:S(2)}) copy-start(f32[8,1024]{1,0:T(8,128)} %copy-done.10) | copy-start | bytes 98308
  166.2 5.2 %copy-start.7 = (s32[1024]{0:T(1024)S(1)}, s32[1024]{0:T(1024)}, u32[]{:S(2)}) copy-start(s32[1024]{0:T(1024)} %copy-done.6) | copy-start | bytes 12292
  (6 other events, 16.3 us)
